TPU v7x, 32 devices: a whole 2x2x4 slice. The times are simulated.
32 devices in a mesh: groups: 2 (over y), sol: 4 (over z), head: 2 (over x), sub: 2 (over core).
Axes of the slice: x: 2, y: 2, z: 4, core: 2. Of those that a mesh axis runs over, the one named last changes fastest.
Arguments:
- query_key: bfloat16 [16, 512, 2, 2048], P(('groups', 'sol'), None, None, ('head', 'sub')), parts along dimension 0, may hold values from -6 to 6
- values_in: bfloat16 [16, 512, 4096], P(('groups', 'sol'), None, ('head', 'sub')), parts along dimension 0, may hold values from -6 to 6
- gate_in: bfloat16 [16, 512, 4096], P(('groups', 'sol'), None, ('head', 'sub')), parts along dimension 0, may hold values from -6 to 6
- decay_in: float32 [16, 32, 512], P(('groups', 'sol'), ('head', 'sub')), parts along dimension 0, may hold values from -6 to 6
- beta_in: float32 [16, 32, 512], P(('groups', 'sol'), ('head', 'sub')), parts along dimension 0, may hold values from -6 to 6
- decay_rate: float32 [32], P(('head', 'sub')), may hold values from 0.002 to 0.08
- decay_bias: float32 [32], P(('head', 'sub')), may hold values from -1 to 1
- conv_qk: float32 [4, 2, 2048], P(None, None, ('head', 'sub')), may hold values from -3 to 3
- conv_v: float32 [4, 4096], P(None, ('head', 'sub')), may hold values from -3 to 3
- prompt_states: bfloat16 [8, 32, 128, 128], P(('groups', 'sol'), ('head', 'sub')), parts along dimension 0, may hold values from -6 to 6
- prompt_of: int32 [16], P(('groups', 'sol')), parts along dimension 0, may hold values from 0 to 3
- step_ends: int32 [16, 2], P(('groups', 'sol')), parts along dimension 0, may hold values from 1 to 512, as said below
- norm_gain: float32 [128], replicated, may hold values from 0.25 to 1.75
- probe: bfloat16 [4096], replicated, may hold values from -0.09375 to 0.09375
Outputs:
- hidden: bfloat16 [16, 512, 4096], P(('groups', 'sol'), ('head', 'sub')), parts along dimension 0
- step_logits: float32 [16, 2], P(('groups', 'sol')), parts along dimension 0
There are 2 independent parts, one for each index of `groups`. A program takes and returns all parts, laid end to end along the dimension named above; an argument that names none is the same for every part. Nothing has to cross between parts.
Inputs may be any that keep to these rules, and one draw needn't show every extreme that they name: Solution s continues prompt prompt_of[s]. step_ends[s,0] < step_ends[s,1]; the first step covers positions below step_ends[s,0], the second the positions from there below step_ends[s,1]; later positions are padding. Some solution has step_ends[s,1] = 512.
All inputs are finite; a program needn't handle non-finite values.
Results may differ from a plain program's by a relative error of at most 0.0032.
Values may be sent and summed in bfloat16 or wider, within the bound.
A program may use at most 128 MiB of HBM per device.

v0:
```python
import jax
import jax.numpy as jnp
from jax import lax
from jax.sharding import PartitionSpec as P

BLOCK = 128


def conv_silu(inputs, kernel):
    width = kernel.shape[0]
    count = inputs.shape[1]
    padded = jnp.pad(inputs, ((0, 0), (width - 1, 0), (0, 0)))
    total = jnp.zeros(inputs.shape, jnp.float32)
    for offset in range(width):
        total = total + padded[:, offset : offset + count, :] * kernel[offset]
    return jax.nn.silu(total)


def unit_rows(field, head_size):
    shape = field.shape
    split = field.reshape(shape[:-1] + (shape[-1] // head_size, head_size))
    return split / jnp.sqrt(jnp.sum(split * split, axis=-1, keepdims=True) + 1e-06)


def pick_states(owners, block):
    labels = jnp.arange(block.shape[0], dtype=jnp.int32)
    select = (owners[:, None] == labels[None, :]).astype(jnp.bfloat16)
    return jnp.einsum("sp,phkv->shkv", select, block, preferred_element_type=jnp.float32)


def delta_blocks(queries, keys, values, log_decay, beta, initial):
    sols, length, heads, size = queries.shape
    count = length // BLOCK
    highest = lax.Precision.HIGHEST

    def blocks(field):
        return field.reshape(sols, count, BLOCK, heads, size).transpose(1, 0, 3, 2, 4)

    def gates(field):
        return field.reshape(sols, heads, count, BLOCK).transpose(2, 0, 1, 3)

    query_blocks = blocks(queries)
    key_blocks = blocks(keys)
    value_blocks = blocks(values)
    cumulative = jnp.cumsum(gates(log_decay), axis=-1)
    rate = gates(beta)
    places = jnp.arange(BLOCK)
    within = places[:, None] >= places[None, :]
    strict = places[:, None] > places[None, :]
    spread = cumulative[..., :, None] - cumulative[..., None, :]
    weights = jnp.where(within, jnp.exp(jnp.where(within, spread, 0.0)), 0.0)
    key_gram = jnp.einsum("nshid,nshjd->nshij", key_blocks, key_blocks, precision=highest)
    system = jnp.eye(BLOCK, dtype=jnp.float32) + jnp.where(
        strict, rate[..., :, None] * key_gram * weights, 0.0
    )
    right = jnp.concatenate(
        [rate[..., None] * value_blocks, (rate * jnp.exp(cumulative))[..., None] * key_blocks],
        axis=-1,
    )
    solved = jax.scipy.linalg.solve_triangular(system, right, lower=True, unit_diagonal=True)
    updates = solved[..., :size]
    corrections = solved[..., size:]
    scores = jnp.einsum("nshid,nshjd->nshij", query_blocks, key_blocks, precision=highest) * weights

    def advance(state, inputs):
        query, key, update, correction, score, cumul = inputs
        fresh = update - jnp.einsum("shck,shkv->shcv", correction, state, precision=highest)
        output = jnp.exp(cumul)[..., None] * jnp.einsum(
            "shck,shkv->shcv", query, state, precision=highest
        )
        output = output + jnp.einsum("shij,shjv->shiv", score, fresh, precision=highest)
        last = cumul[..., -1:]
        tail = jnp.exp(last - cumul)
        state = jnp.exp(last)[..., None] * state + jnp.einsum(
            "shck,shcv->shkv", key * tail[..., None], fresh, precision=highest
        )
        return (state, output)

    unused, outputs = lax.scan(
        advance, initial, (query_blocks, key_blocks, updates, corrections, scores, cumulative)
    )
    return outputs.transpose(1, 0, 3, 2, 4).reshape(sols, length, heads * size)


def gated_norm(core, gate, gain, first, ends):
    sols, count, width = core.shape
    size = gain.shape[0]
    split = core.reshape(sols, count, width // size, size)
    scale = jnp.sqrt(jnp.mean(split * split, axis=-1, keepdims=True) + 1e-06)
    normed = split / scale * gain * jax.nn.silu(gate.reshape(split.shape).astype(jnp.float32))
    places = first + jnp.arange(count, dtype=jnp.int32)
    live = places[None, :] < ends[:, 1:2]
    hidden = jnp.where(live[:, :, None], normed.reshape(sols, count, width), 0.0).astype(
        jnp.bfloat16
    )
    return (hidden, places)


def end_terms(hidden, probe_part, places, ends):
    sols, count, width = hidden.shape
    reward = jnp.dot(
        hidden.reshape(sols * count, width), probe_part, preferred_element_type=jnp.float32
    ).reshape(sols, count)
    marked = places[None, :, None] == (ends - 1)[:, None, :]
    return jnp.sum(jnp.where(marked, reward[:, :, None], 0.0), axis=1)


def shuffle_pair(core, gate):
    moved_core, moved_gate = (
        lax.all_to_all(core, ("head", "sub"), split_axis=1, concat_axis=2, tiled=True),
        lax.all_to_all(
            gate.astype(jnp.float32), ("head", "sub"), split_axis=1, concat_axis=2, tiled=True
        ).astype(gate.dtype),
    )
    return (moved_core, moved_gate)


def on_device(
    query_key,
    values_in,
    gate_in,
    decay_in,
    beta_in,
    decay_rate,
    decay_bias,
    conv_qk,
    conv_v,
    prompt_states,
    prompt_of,
    step_ends,
    norm_gain,
    probe,
):
    sols, length = (query_key.shape[0], query_key.shape[1])
    key_width = query_key.shape[3]
    head_size = prompt_states.shape[-1]
    value_heads = prompt_states.shape[1]
    mixed = conv_silu(
        query_key.reshape(sols, length, 2 * key_width),
        conv_qk.reshape(conv_qk.shape[0], 2 * key_width),
    )
    queries = unit_rows(mixed[:, :, :key_width], head_size) * head_size ** (-0.5)
    keys = unit_rows(mixed[:, :, key_width:], head_size)
    repeat = value_heads // queries.shape[2]
    queries = jnp.repeat(queries, repeat, axis=2)
    keys = jnp.repeat(keys, repeat, axis=2)
    values = conv_silu(values_in, conv_v).reshape(sols, length, value_heads, head_size)
    log_decay = -decay_rate[None, :, None] * jax.nn.softplus(decay_in + decay_bias[None, :, None])
    beta = jax.nn.sigmoid(beta_in)
    every = lax.all_gather(prompt_states, "sol", axis=0, tiled=True)
    initial = pick_states(prompt_of, every)
    core = delta_blocks(queries, keys, values, log_decay, beta, initial)
    moved_core, moved_gate = shuffle_pair(core, gate_in)
    share = length // lax.axis_size(("head", "sub"))
    hidden, places = gated_norm(
        moved_core, moved_gate, norm_gain, lax.axis_index(("head", "sub")) * share, step_ends
    )
    partial_value = end_terms(hidden, probe, places, step_ends)
    step_logits = lax.psum(partial_value, ("head", "sub"))
    return (hidden, step_logits)


def solution(mesh):
    return jax.shard_map(
        on_device,
        mesh=mesh,
        in_specs=(
            P(("groups", "sol"), None, None, ("head", "sub")),
            P(("groups", "sol"), None, ("head", "sub")),
            P(("groups", "sol"), None, ("head", "sub")),
            P(("groups", "sol"), ("head", "sub"), None),
            P(("groups", "sol"), ("head", "sub"), None),
            P(("head", "sub")),
            P(("head", "sub")),
            P(None, None, ("head", "sub")),
            P(None, ("head", "sub")),
            P(("groups", "sol"), ("head", "sub"), None, None),
            P(("groups", "sol")),
            P(("groups", "sol"), None),
            P(),
            P(),
        ),
        out_specs=(P(("groups", "sol"), ("head", "sub"), None), P(("groups", "sol"), None)),
        check_vma=False,
    )
```

profile of v0, /device:TPU:11, one launch (start us, length us, event | category | flops | bytes accessed | tf_op | source)
XLA Modules:
  0.0 894.4 jit_solution(11144132423608465836)
XLA Ops:
  7.9 5.1 copy.128
  13.0 5.8 all-to-all-start.1
  18.9 3.3 reshape.201
  22.2 2.8 divide_multiply_fusion.1
  25.0 2.6 fusion.49
  27.6 1.9 reshape.202
  29.5 1.2 multiply_reduce_fusion.1
  30.9 1.4 broadcast_divide_fusion
  32.5 2.8 divide_multiply_fusion
  35.3 2.9 copy.143
  38.4 2.3 reduce_window_sum.11
  41.2 1.9 copy-done.1
  43.1 11.1 %add_bitcast_fusion = f32[4,2,8,1,128,128]{5,4,3,2,1,0:T(8,128)} fusion(f32[128,128]{1,0:T(8,128)S(1)} %get-tuple-element.149, f32[4,2,8,128]{3,2,1,0:T(8,128)S(1)} %reduce_window_sum.11, f32[4,2,8,128]{3,2,1,0:T(8,128)S(1)} %copy_bitcast_fusion, f32[128,128]{1,0:T(8,128)S(1)} %get-tuple-element.148, pred[128,128]{1,0:T(8,128)(4,1)S(1)} %iota_compare_fusion.1, ...), kind=kOutput, calls=%fused_computation.44 | convolution fusion | flops 1620049920 | bytes 8634368 | tf_op jit(solution)/shard_map/nshid,nshjd->nshij/dot_general | solution.py:52
  54.2 630.3 %custom-call.4 = f32[4,2,8,1,128,128]{4,5,3,2,1,0:T(8,128)} custom-call(f32[4,2,8,1,128,128]{5,4,3,2,1,0:T(8,128)} %add_bitcast_fusion), custom_call_target="InvertDiagBlocksLowerTriangular" | custom-call | tf_op jit(solution)/shard_map/jit(_solve_triangular)/vmap(vmap(vmap()))/triangular_solve | solution.py:60
  684.5 2.1 reshape.204
  686.6 1.2 multiply_reduce_fusion
  687.9 1.5 divide_multiply_fusion.2
  690.1 2.0 copy-done.4
  692.1 2.2 copy.122
  694.3 5.2 bitcast_multiply_fusion.3
  699.5 10.3 %fusion.12 = f32[4,2,8,128,256]{4,3,2,1,0:T(8,128)S(1)} fusion(f32[4,2,8,128,128]{4,3,2,1,0:T(8,128)S(1)} %get-tuple-element.151, f32[4,2,8,128,128]{4,3,2,1,0:T(8,128)S(1)} %get-tuple-element.150, f32[4,2,8,1,128,128]{4,5,3,2,1,0:T(8,128)} %custom-call.4), kind=kOutput, calls=%fused_computation.23 | convolution fusion | flops 3223322624 | bytes 20971520 | tf_op jit(solution)/shard_map/jit(_solve_triangular)/vmap(vmap(vmap()))/triangular_solve | solution.py:60
  709.8 5.3 fusion.48
  715.1 1.1 copy-done.5
  716.2 10.6 %fusion.27 = f32[4,2,8,128,128]{4,3,2,1,0:T(8,128)} fusion(f32[4,2,8,128]{3,2,1,0:T(8,128)S(1)} %reduce_window_sum.11, pred[128,128]{1,0:T(8,128)(4,1)S(1)} %iota_compare_fusion.1, f32[2,4,128,8,128]{4,2,1,3,0:T(8,128)S(1)} %bitcast.180, f32[4,2,8,128,128]{4,3,0,2,1:T(8,128)S(1)} %bitcast.185), kind=kOutput, calls=%fused_computation.46 | convolution fusion | flops 1614807040 | bytes 12632064 | tf_op jit(solution)/shard_map/nshid,nshjd->nshij/dot_general | solution.py:63
  726.8 2.2 fusion.35
  729.1 58.6 %while.13 = (s32[]{:T(128)}, f32[2,8,128,128]{3,2,1,0:T(8,128)S(1)}, f32[4,2,8,128,128]{4,3,2,1,0:T(8,128)}, f32[4,2,8,128]{3,2,1,0:T(8,128)S(1)}, f32[4,2,8,128...) while((s32[]{:T(128)}, ...), condition=%wide.region_4.5_spmd.clone, body=%wide.region_3.4_spmd.sunk.clone | while | flops 1612187648 | bytes 20032420 | solution.py:79
  729.5 2.5 convolution_multiply_fusion.3
  732.0 2.8 convolution_subtract_fusion.3
  734.9 3.4 fusion.82
  738.3 2.3 constant_dynamic-slice_fusion.6
  740.6 1.6 copy.174
  742.2 1.6 convolution_add_fusion.4
  744.2 2.5 convolution_multiply_fusion.3
  746.7 2.8 convolution_subtract_fusion.3
  749.5 3.4 fusion.82
  752.9 2.3 constant_dynamic-slice_fusion.6
  755.3 1.6 copy.174
  756.8 1.6 convolution_add_fusion.4
  758.8 2.5 convolution_multiply_fusion.3
  761.3 2.8 convolution_subtract_fusion.3
  764.1 3.4 fusion.82
  767.6 2.3 constant_dynamic-slice_fusion.6
  769.9 1.6 copy.174
  771.5 1.6 convolution_add_fusion.4
  773.4 2.5 convolution_multiply_fusion.3
  775.9 2.8 convolution_subtract_fusion.3
  778.7 3.4 fusion.82
  782.2 2.3 constant_dynamic-slice_fusion.6
  784.6 1.6 copy.174
  786.1 1.6 convolution_add_fusion.4
  787.7 6.6 copy.135
  794.3 5.8 reshape.212
  800.1 5.3 all-to-all-start
  805.7 6.7 copy.129
  812.5 39.2 %all-to-all-done = f32[2,512,1024]{2,0,1:T(2,128)} async-done(((f32[2,512,1024]{2,0,1:T(2,128)}), f32[2,512,1024]{2,0,1:T(2,128)}, u32[]{:S(2)}, u32[]{:S(2)}) %all-to-all-start) | async-done | bytes 4194336 | tf_op jit(solution)/shard_map/all_to_all | solution.py:110
  851.7 3.5 copy.125
  855.2 1.9 copy-done.3
  857.2 2.9 mul.258
  860.0 5.4 copy.126
  865.5 5.4 copy.127
  870.9 2.7 reduce_sum.38
  873.5 4.3 fusion.28
  878.4 2.7 copy.130
  881.1 6.2 psum.7
  (87 shorter events, 5.2 us)
Async XLA Ops:
  7.2 798.5 %copy-start = (f32[128]{0:T(128)S(1)}, f32[128]{0:T(128)}, u32[]{:S(2)}) copy-start(f32[128]{0:T(128)} %param.28) | copy-start | bytes 1540
  7.2 719.6 %all-gather.2.cloned.1.call-start = ((), (), s32[]{:S(2)}) async-start(), calls=%async_computation.2 | async-start | bytes 1310720 | tf_op jit(solution)/shard_map/all_gather | solution.py:150
  7.9 11.0 %copy-start.9 = (f32[4,2,512]{2,1,0:T(2,128)S(1)}, f32[4,2,512]{2,1,0:T(2,128)}, u32[]{:S(2)}) copy-start(f32[4,2,512]{2,1,0:T(2,128)} %param.23) | copy-start | bytes 49156
  13.0 787.1 %all-to-all-start.1 = ((bf16[2,512,1024]{2,0,1:T(2,128)(2,1)}), bf16[2,512,1024]{2,0,1:T(2,128)(2,1)}, u32[]{:S(2)}, u32[]{:S(2)}) async-start(bf16[2,512,1024]{2,0,1:T(2,128)(2,1)} %copy.128), calls=%async_computation.1 | async-start | bytes 4194304 | tf_op jit(solution)/shard_map/all_to_all | solution.py:111
  30.8 1.6 copy-start.10
  30.9 1.6 copy-start.6
  35.2 3.0 copy-start.15
  35.3 3.0 copy-start.7
  35.3 3.0 copy-start.8
  35.3 3.0 copy-start.13
  41.2 2.0 copy-start.1
  690.1 2.0 copy-start.4
  709.8 5.3 copy-start.2
  709.8 6.4 copy-start.5
  716.2 10.7 %copy-start.14 = (s32[2]{0:T(128)S(1)}, s32[2]{0:T(128)}, u32[]{:S(2)}) copy-start(s32[2]{0:T(128)} %param.26) | copy-start | bytes 28
  800.1 5.3 copy-start.11
  800.1 5.4 copy-start.12
  800.1 51.6 %all-to-all-start = ((f32[2,512,1024]{2,0,1:T(2,128)}), f32[2,512,1024]{2,0,1:T(2,128)}, u32[]{:S(2)}, u32[]{:S(2)}) async-start(f32[2,512,1024]{2,0,1:T(2,128)} %reshape.212), calls=%async_computation | async-start | bytes 8388608 | tf_op jit(solution)/shard_map/all_to_all | solution.py:110
  855.2 1.9 copy-start.3
Sparse Core Ops, SparseCore 0:
  9.6 28.8 all-gather.1
where the time goes:
time: 900 us; the launch traced here: 894 us
  other arithmetic  660 us (73%)
  local copies, waits for them, and re-layouts  86.7 us (10%)
  matrix products  75.6 us (8%)
  waiting for transfers between devices  39.9 us (4%)
  between operations  14.8 us (2%)
  starting transfers between devices  11.1 us (1%)
    another operation x2, other arithmetic, delta_blocks(): jax.scipy.linalg.solve_triangular(system, right, lower=True, unit_diagona...  630 us
    all_to_all x1, waiting for transfers between devices, shuffle_pair(): lax.all_to_all(core, ('head', 'sub'), split_axis=1, concat_axis=2, tiled=...  39.2 us
  transfers between devices with their start and end apart: 3, of which 1 were waited for; matrix products, arithmetic and copies ran while one was open for 88% of the time, Pallas kernels for 0%

commit v1 on v0

v1 whole, which is shorter than its diff:
```python
import functools

import jax
import jax.numpy as jnp
from jax import lax
from jax.experimental import pallas as pl
from jax.experimental.pallas import tpu as pltpu
from jax.sharding import PartitionSpec as P

C = 128
F32 = jnp.float32
BF16 = jnp.bfloat16


def dot(a, b):
    return lax.dot_general(a, b, (((1,), (0,)), ((), ())), preferred_element_type=F32)


def split(x):
    high = x.astype(BF16)
    return high, (x - high.astype(F32)).astype(BF16)


def pack(x):
    return jnp.concatenate(split(x), axis=1)


def pack_right(x):
    row = pack(x)
    return jnp.concatenate([row, row], axis=0)


def packed_dot(left, right):
    both = dot(left, right)
    return both[:, :C] + both[:, C:]


def silu(x):
    return x / (1.0 + jnp.exp(-x))


def conv_silu(x, taps):
    rows = lax.broadcasted_iota(jnp.int32, x.shape, 0)
    total = x * taps[3:4]
    for back in range(1, 4):
        moved = jnp.where(rows >= back, pltpu.roll(x, back, 0), 0.0)
        total = total + moved * taps[3 - back : 4 - back]
    return silu(total)


def unit(x):
    return x * lax.rsqrt(jnp.sum(x * x, axis=-1, keepdims=True) + 1e-06)


def kernel(
    ends_ref, owner_ref, qk_ref, v_ref, gate_ref, decay_ref, beta_ref, rate_ref, bias_ref, tqk_ref, tv_ref,
    init_ref, gain_ref, hid_ref, sel_ref, rows_ref, kq_ref, kt_ref, x_ref, score_ref, vb_ref, s_ref,
):
    sols, length, width = v_ref.shape
    heads = width // C
    groups = heads // 2
    count = length // C
    ii = lax.broadcasted_iota(jnp.int32, (C, C), 0)
    jj = lax.broadcasted_iota(jnp.int32, (C, C), 1)
    ones = jnp.where(ii <= jj, 1.0, 0.0).astype(F32)

    def one_solution(s, carry):
        log_decay = -rate_ref[...] * jax.nn.softplus(decay_ref[s] + bias_ref[...])
        beta = jax.nn.sigmoid(beta_ref[s])
        for c in range(count):
            cols = slice(c * C, (c + 1) * C)
            cum = lax.dot_general(
                log_decay[:, cols], ones, (((1,), (0,)), ((), ())),
                precision=lax.Precision.HIGHEST, preferred_element_type=F32,
            )
            for g in range(groups):
                pair = slice(2 * g, 2 * g + 2)
                rows_ref[g, c] = jnp.concatenate(
                    [cum[pair], beta[pair, cols], jnp.zeros((4, C), F32)], axis=0
                )

        def prepare(g, carry):
            at = pl.ds(pl.multiple_of(g * C, C), C)
            at2 = pl.ds(pl.multiple_of(width // 2 + g * C, C), C)
            q = unit(conv_silu(qk_ref[s, :, at].astype(F32), tqk_ref[:, at])) * C ** (-0.5)
            k = unit(conv_silu(qk_ref[s, :, at2].astype(F32), tqk_ref[:, at2]))
            atv = pl.ds(pl.multiple_of(g * 2 * C, 2 * C), 2 * C)
            v = conv_silu(v_ref[s, :, atv].astype(F32), tv_ref[:, atv])
            systems = []
            for c in range(count):
                span = slice(c * C, (c + 1) * C)
                kt = jnp.transpose(k[span])
                kth, ktl = split(kt)
                ktp = jnp.concatenate([kth, ktl], axis=1)
                kt_ref[g, c] = ktp
                kqp = jnp.concatenate([pack(k[span]), pack(q[span])], axis=0)
                kq_ref[g, c] = kqp
                gram = packed_dot(kqp, jnp.concatenate([ktp, ktp], axis=0))
                rows = rows_ref[g, c]
                cols = jnp.transpose(rows)
                for h in range(2):
                    spread = cols[:, h : h + 1] - rows[h : h + 1, :]
                    weights = jnp.exp(jnp.where(ii >= jj, spread, -1e30))
                    rate = cols[:, 2 + h : 3 + h]
                    score_ref[g, c, h] = pack(gram[C:] * weights)
                    systems.append(jnp.where(ii > jj, rate * gram[:C] * weights, 0.0))
                    vb_ref[g, c, :, h * C : (h + 1) * C] = rate * v[span, h * C : (h + 1) * C]
            far = ii ^ jj
            eye = jnp.where(ii == jj, 1.0, 0.0)
            inverses = [eye - jnp.where(far == 1, m, 0.0) for m in systems]
            b = 2
            while b < C:
                near = (far >= b) & (far < 2 * b)
                packs = [pack(x) for x in inverses]
                mids = [
                    packed_dot(p, pack_right(jnp.where(near, m, 0.0)))
                    for p, m in zip(packs, systems)
                ]
                inverses = [
                    x - packed_dot(pack(y), jnp.concatenate([p, p], axis=0))
                    for x, y, p in zip(inverses, mids, packs)
                ]
                b *= 2
            for c in range(count):
                for h in range(2):
                    x_ref[g, c, h] = pack(inverses[2 * c + h])
            return carry

        lax.fori_loop(0, groups, prepare, 0)

        for g in range(groups):
            for h in range(2):
                s_ref[g, :, h * C : (h + 1) * C] = init_ref[owner_ref[s], 2 * g + h].astype(F32)

        def advance(c, carry):
            span = pl.ds(pl.multiple_of(c * C, C), C)
            place = c * C + lax.broadcasted_iota(jnp.int32, (C, 1), 0)
            live = place < ends_ref[s, 1]
            row = lax.broadcasted_iota(jnp.int32, (8, C), 0)
            lane = c * C + lax.broadcasted_iota(jnp.int32, (8, C), 1)
            pick = jnp.where(
                ((row == 0) & (lane == ends_ref[s, 0] - 1)) | ((row == 1) & (lane == ends_ref[s, 1] - 1)),
                1.0, 0.0,
            ).astype(BF16)
            for g in range(groups):
                state = s_ref[g]
                sh, sl = split(state)
                kqp = kq_ref[g, c]
                reads = dot(kqp, jnp.concatenate([sh, sh], axis=0)) + dot(kqp[:, :C], sl)
                rows = rows_ref[g, c]
                cols = jnp.transpose(rows)
                tails, keeps = [], []
                for h in range(2):
                    part = slice(h * C, (h + 1) * C)
                    cum = cols[:, h : h + 1]
                    grown = jnp.exp(cum)
                    last = rows[h : h + 1, C - 1 : C]
                    right = vb_ref[g, c, :, part] - (cols[:, 2 + h : 3 + h] * grown) * reads[:C, part]
                    fresh = packed_dot(x_ref[g, c, h], pack_right(right))
                    core = grown * reads[C:, part] + packed_dot(score_ref[g, c, h], pack_right(fresh))
                    tails.append(fresh * jnp.exp(last - cum))
                    keeps.append(jnp.exp(last) * state[:, part])
                    scale = lax.rsqrt(jnp.mean(core * core, axis=-1, keepdims=True) + 1e-06)
                    chan = pl.ds((2 * g + h) * C, C)
                    gate = gate_ref[s, span, chan].astype(F32)
                    out = core * scale * gain_ref[...] * silu(gate)
                    hid = jnp.where(live, out, 0.0).astype(BF16)
                    share = length // hid_ref.shape[0]
                    for d in range(C // share):
                        hid_ref[c * (C // share) + d, s, :, chan] = hid[d * share : (d + 1) * share]
                    chosen = dot(pick, hid)
                    old = jnp.where(c == 0, 0.0, sel_ref[s, :, chan])
                    sel_ref[s, :, chan] = old + chosen
                fresh = jnp.concatenate(tails, axis=1)
                fh, fl = split(fresh)
                ktp = kt_ref[g, c]
                s_ref[g] = (
                    jnp.concatenate(keeps, axis=1)
                    + dot(ktp, jnp.concatenate([fh, fh], axis=0))
                    + dot(ktp[:, :C], fl)
                )
            return carry

        lax.fori_loop(0, count, advance, 0)
        return carry

    lax.fori_loop(0, sols, one_solution, 0)


def run_layer(ends, owner, qk, v, gate, decay, beta, rate, bias, tqk, tv, init, gain):
    sols, length, width = v.shape
    groups = width // C // 2
    count = length // C
    shares = lax.axis_size(("head", "sub"))
    vmem = pl.BlockSpec(memory_space=pltpu.VMEM)
    return pl.pallas_call(
        kernel,
        out_shape=(
            jax.ShapeDtypeStruct((shares, sols, length // shares, width), BF16),
            jax.ShapeDtypeStruct((sols, 8, width), F32),
        ),
        in_specs=[pl.BlockSpec(memory_space=pltpu.SMEM)] * 2 + [vmem] * 11,
        out_specs=(vmem, vmem),
        scratch_shapes=[
            pltpu.VMEM((groups, count, 8, C), F32),
            pltpu.VMEM((groups, count, 2 * C, 2 * C), BF16),
            pltpu.VMEM((groups, count, C, 2 * C), BF16),
            pltpu.VMEM((groups, count, 2, C, 2 * C), BF16),
            pltpu.VMEM((groups, count, 2, C, 2 * C), BF16),
            pltpu.VMEM((groups, count, C, 2 * C), F32),
            pltpu.VMEM((groups, C, 2 * C), F32),
        ],
        compiler_params=pltpu.CompilerParams(vmem_limit_bytes=56 * 1024 * 1024),
        name="delta_layer",
    )(ends, owner, qk, v, gate, decay, beta, rate, bias, tqk, tv, init, gain)


def on_device(
    query_key, values_in, gate_in, decay_in, beta_in, decay_rate, decay_bias, conv_qk, conv_v,
    prompt_states, prompt_of, step_ends, norm_gain, probe,
):
    sols, length, _, key_width = query_key.shape
    width = values_in.shape[2]
    every = lax.all_gather(prompt_states, "sol", axis=0, tiled=True)
    hidden, chosen = run_layer(
        step_ends, prompt_of,
        query_key.reshape(sols, length, 2 * key_width),
        values_in, gate_in, decay_in, beta_in, decay_rate[:, None], decay_bias[:, None],
        conv_qk.reshape(conv_qk.shape[0], 2 * key_width), conv_v, every, norm_gain[None, :],
    )
    me = lax.axis_index(("head", "sub"))
    part = lax.dynamic_slice_in_dim(probe, me * width, width, 0).astype(F32)
    logits = lax.psum(jnp.sum(chosen[:, :2] * part, axis=-1), ("head", "sub"))
    moved = lax.all_to_all(hidden, ("head", "sub"), split_axis=0, concat_axis=0, tiled=True)
    share = length // hidden.shape[0]
    return moved.transpose(1, 2, 0, 3).reshape(sols, share, hidden.shape[0] * width), logits


def solution(mesh):
    return jax.shard_map(
        on_device,
        mesh=mesh,
        in_specs=(
            P(("groups", "sol"), None, None, ("head", "sub")),
            P(("groups", "sol"), None, ("head", "sub")),
            P(("groups", "sol"), None, ("head", "sub")),
            P(("groups", "sol"), ("head", "sub"), None),
            P(("groups", "sol"), ("head", "sub"), None),
            P(("head", "sub")),
            P(("head", "sub")),
            P(None, None, ("head", "sub")),
            P(None, ("head", "sub")),
            P(("groups", "sol"), ("head", "sub"), None, None),
            P(("groups", "sol")),
            P(("groups", "sol"), None),
            P(),
            P(),
        ),
        out_specs=(P(("groups", "sol"), ("head", "sub"), None), P(("groups", "sol"), None)),
        check_vma=False,
    )
```

time: 900 us -> 152 us (0.17)
  the two profiles are of different devices: /device:TPU:11 before, /device:TPU:0 now
where the time goes in v1:
time: 152 us; the launch traced here: 151 us
  Pallas kernels  66.4 us (44%)
  waiting for transfers between devices  26.6 us (18%)
  blocking collectives  26 us (17%)
  between operations  14.1 us (9%)
  local copies, waits for them, and re-layouts  13 us (9%)
  starting transfers between devices  3.64 us (2%)
  other arithmetic  1.62 us (1%)
    pallas_call x1, Pallas kernels, run_layer(): pl.pallas_call(kernel, out_shape=(jax.ShapeDtypeStruct((shares, sols, len...  66.4 us
    psum x1, blocking collectives, on_device(): logits = lax.psum(jnp.sum(chosen[:, :2] * part, axis=-1), ('head', 'sub'))  26 us
    all_gather x1, waiting for transfers between devices, on_device(): every = lax.all_gather(prompt_states, 'sol', axis=0, tiled=True)  25.9 us
    unnamed x8, local copies, waits for them, and re-layouts  4.68 us
    reshape x1, local copies, waits for them, and re-layouts, on_device(): query_key.reshape(sols, length, 2 * key_width)  4.44 us
    all_to_all x1, starting transfers between devices, on_device(): lax.all_to_all(hidden, ('head', 'sub'), split_axis=0, concat_axis=0, tile...  3.61 us
  transfers between devices with their start and end apart: 2, of which 1 were waited for; matrix products, arithmetic and copies ran while one was open for 5% of the time, Pallas kernels for 0%

profile of v1, /device:TPU:0, one launch (start us, length us, event | category | flops | bytes accessed | tf_op | source)
XLA Modules:
  0.0 151.4 jit_solution(13386295634134237305)
XLA Ops:
  7.2 0.0 all-gather.2.cloned.1.call-start
  7.2 0.7 all-gather.2.cloned.1.call-update
  7.9 0.0 copy-start.1
  7.9 0.0 copy-start.2
  7.9 0.0 copy-start
  7.9 4.4 %reshape.14.qk_ref = bf16[2,512,1024]{2,1,0:T(8,128)(2,1)} reshape(bf16[2,512,2,512]{3,2,1,0:T(2,128)(2,1)} %param.14) | data formatting | bytes 4194304 | tf_op jit(solution)/shard_map/reshape | solution.py:227
  12.4 0.0 copy-done.1
  12.4 0.7 copy.22.rate_ref
  13.0 0.0 copy-done.2
  13.0 0.7 copy.23.bias_ref
  13.7 0.0 copy-done
  13.7 0.6 copy.26
  14.3 25.9 %all-gather.2.cloned.1.call-done.init_ref = bf16[4,8,128,128]{3,2,1,0:T(8,128)(2,1)} async-done(((bf16[1,8,128,128]{3,2,1,0:T(8,128)(2,1)}), bf16[4,8,128,128]{3,2,1,0:T(8,128)(2,1)}) %all-gather.2.cloned.1.call-update) | async-done | bytes 1048592 | tf_op jit(solution)/shard_map/all_gather | solution.py:224
  40.2 66.4 %delta_layer.1 = (bf16[4,2,128,1024]{3,2,1,0:T(8,128)(2,1)}, f32[2,8,1024]{2,1,0:T(8,128)}) custom-call(s32[2,2]{1,0:T(2,128)} %ends_ref.1, s32[2]{0:T(128)} %owner_ref.1, bf16[2,512,1024]{2,1,0:T(8,128)(2,1)} %reshape.14.qk_ref, bf16[2,512,1024]{2,1,0:T(8,128)(2,1)} %v_ref.1, bf16[2,512,1024]{2,1,0:T(8,128)(2,1)} %gate_ref.1, f32[2,8,512]{2,1,0:T(8,128)} %decay_ref.1, ...), custom_call_target="tpu_custom_call" | custom-call | tf_op jit(solution)/shard_map/delta_layer/pallas_call | solution.py:196
  106.6 3.6 %all-to-all-start = ((bf16[4,2,128,1024]{3,2,1,0:T(8,128)(2,1)}), bf16[4,2,128,1024]{3,2,1,0:T(8,128)(2,1)S(1)}, u32[]{:S(2)}, u32[]{:S(2)}) async-start(bf16[4,2,128,1024]{3,2,1,0:T(8,128)(2,1)} %get-tuple-element.4), calls=%async_computation | async-start | bytes 4194304 | tf_op jit(solution)/shard_map/all_to_all | solution.py:234
  110.2 0.7 dynamic-slice_convert_fusion
  110.9 0.9 multiply_reduce_fusion
  111.9 26.0 %psum.7 = f32[2,2]{1,0:T(2,128)} all-reduce(f32[2,2]{1,0:T(2,128)S(1)} %multiply_reduce_fusion), channel_id=1, replica_groups=mesh['groups'=2,'sol'=4,'head'=2,'sub'=2] {'head','sub'}, use_global_device_ids=true, to_apply=%region_1.0 | all-reduce | flops 4 | bytes 32 | tf_op jit(solution)/shard_map/psum | solution.py:233
  137.9 0.0 all-to-all-done
  137.9 2.6 %copy.24 = bf16[2,128,4,1024]{1,3,2,0:T(8,128)(2,1)} copy(bf16[2,128,4,1024]{3,1,0,2:T(8,128)(2,1)S(1)} %bitcast.7) | data formatting | bytes 4194304 | tf_op jit(solution)/shard_map/transpose | solution.py:236
  140.5 4.1 %copy.25 = bf16[2,128,4096]{2,1,0:T(8,128)(2,1)} copy(bf16[2,128,4096]{1,2,0:T(8,128)(2,1)} %bitcast.8) | data formatting | bytes 4194304
Async XLA Ops:
  7.2 33.1 %all-gather.2.cloned.1.call-start = ((), (), s32[]{:S(2)}) async-start(), calls=%async_computation.1 | async-start | bytes 1310720 | tf_op jit(solution)/shard_map/all_gather | solution.py:224
  7.9 4.5 %copy-start.1 = (f32[8]{0:T(128)S(1)}, f32[8]{0:T(128)}, u32[]{:S(2)}) copy-start(f32[8]{0:T(128)} %param.19) | copy-start | bytes 100
  7.9 5.1 %copy-start.2 = (f32[8]{0:T(128)S(1)}, f32[8]{0:T(128)}, u32[]{:S(2)}) copy-start(f32[8]{0:T(128)} %param.20) | copy-start | bytes 100
  7.9 5.8 %copy-start = (f32[4,2,512]{2,1,0:T(2,128)S(1)}, f32[4,2,512]{2,1,0:T(2,128)}, u32[]{:S(2)}) copy-start(f32[4,2,512]{2,1,0:T(2,128)} %param.21) | copy-start | bytes 49156
  106.6 31.3 %all-to-all-start = ((bf16[4,2,128,1024]{3,2,1,0:T(8,128)(2,1)}), bf16[4,2,128,1024]{3,2,1,0:T(8,128)(2,1)S(1)}, u32[]{:S(2)}, u32[]{:S(2)}) async-start(bf16[4,2,128,1024]{3,2,1,0:T(8,128)(2,1)} %get-tuple-element.4), calls=%async_computation | async-start | bytes 4194304 | tf_op jit(solution)/shard_map/all_to_all | solution.py:234
Sparse Core Ops, SparseCore 0:
  9.6 30.6 all-gather.1

commit v2 on v1

--- a/solution.py
+++ b/solution.py
@@ -1,5 +1,3 @@
-import functools
-
 import jax
 import jax.numpy as jnp
 from jax import lax
@@ -10,6 +8,7 @@
 C = 128
 F32 = jnp.float32
 BF16 = jnp.bfloat16
+MESH = pl.DeviceIdType.MESH
 
 
 def dot(a, b):
@@ -54,9 +53,59 @@
 
 def kernel(
     ends_ref, owner_ref, qk_ref, v_ref, gate_ref, decay_ref, beta_ref, rate_ref, bias_ref, tqk_ref, tv_ref,
-    init_ref, gain_ref, hid_ref, sel_ref, rows_ref, kq_ref, kt_ref, x_ref, score_ref, vb_ref, s_ref,
+    own_ref, gain_ref, probe_ref, out_ref, logit_ref, hid_ref, sel_ref, rows_ref, kq_ref, kt_ref, x_ref,
+    score_ref, vb_ref, s_ref, every_ref, part_ref, st_send, st_recv, hid_send, hid_recv, lg_send, lg_recv, local_sem,
 ):
     sols, length, width = v_ref.shape
+    n_sol, n_sub = lax.axis_size("sol"), lax.axis_size("sub")
+    shares = lax.axis_size("head") * n_sub
+    share = length // shares
+    per_chunk = C // share
+    prompts = own_ref.shape[0]
+    my_sol = lax.axis_index("sol")
+    me = lax.axis_index("head") * n_sub + lax.axis_index("sub")
+
+    def mate(index):
+        return {"head": index // n_sub, "sub": index % n_sub}
+
+    barrier = pltpu.get_barrier_semaphore()
+    for r in range(1, n_sol):
+        pl.semaphore_signal(barrier, 1, device_id={"sol": lax.rem(my_sol + r, n_sol)}, device_id_type=MESH)
+    for r in range(1, shares):
+        pl.semaphore_signal(barrier, 1, device_id=mate(lax.rem(me + r, shares)), device_id_type=MESH)
+    pl.semaphore_wait(barrier, n_sol + shares - 2)
+
+    def state_copy(r, slot):
+        return pltpu.make_async_remote_copy(
+            src_ref=own_ref, dst_ref=every_ref.at[pl.ds(slot * prompts, prompts)],
+            send_sem=st_send.at[r - 1], recv_sem=st_recv.at[r - 1],
+            device_id={"sol": lax.rem(my_sol + r, n_sol)}, device_id_type=MESH,
+        )
+
+    def hidden_copy(s, to, source):
+        return pltpu.make_async_remote_copy(
+            src_ref=hid_ref.at[to, s],
+            dst_ref=out_ref.at[s, :, pl.ds(pl.multiple_of(source * width, width), width)],
+            send_sem=hid_send.at[s, to], recv_sem=hid_recv.at[s, source],
+            device_id=mate(to), device_id_type=MESH,
+        )
+
+    def hidden_local(s):
+        return pltpu.make_async_copy(
+            hid_ref.at[me, s], out_ref.at[s, :, pl.ds(pl.multiple_of(me * width, width), width)],
+            local_sem.at[s],
+        )
+
+    def part_copy(r, slot):
+        return pltpu.make_async_remote_copy(
+            src_ref=part_ref.at[slot], dst_ref=part_ref.at[slot],
+            send_sem=lg_send.at[r - 1], recv_sem=lg_recv.at[r - 1],
+            device_id=mate(lax.rem(me + r, shares)), device_id_type=MESH,
+        )
+
+    for r in range(1, n_sol):
+        state_copy(r, my_sol).start()
+    every_ref[pl.ds(my_sol * prompts, prompts)] = own_ref[...]
     heads = width // C
     groups = heads // 2
     count = length // C
@@ -128,9 +177,14 @@
 
         lax.fori_loop(0, groups, prepare, 0)
 
+        @pl.when(s == 0)
+        def _():
+            for r in range(1, n_sol):
+                state_copy(r, lax.rem(my_sol + n_sol - r, n_sol)).wait_recv()
+
         for g in range(groups):
             for h in range(2):
-                s_ref[g, :, h * C : (h + 1) * C] = init_ref[owner_ref[s], 2 * g + h].astype(F32)
+                s_ref[g, :, h * C : (h + 1) * C] = every_ref[owner_ref[s], 2 * g + h].astype(F32)
 
         def advance(c, carry):
             span = pl.ds(pl.multiple_of(c * C, C), C)
@@ -165,9 +219,8 @@
                     gate = gate_ref[s, span, chan].astype(F32)
                     out = core * scale * gain_ref[...] * silu(gate)
                     hid = jnp.where(live, out, 0.0).astype(BF16)
-                    share = length // hid_ref.shape[0]
-                    for d in range(C // share):
-                        hid_ref[c * (C // share) + d, s, :, chan] = hid[d * share : (d + 1) * share]
+                    for d in range(per_chunk):
+                        hid_ref[c * per_chunk + d, s, :, chan] = hid[d * share : (d + 1) * share]
                     chosen = dot(pick, hid)
                     old = jnp.where(c == 0, 0.0, sel_ref[s, :, chan])
                     sel_ref[s, :, chan] = old + chosen
@@ -179,29 +232,63 @@
                     + dot(ktp, jnp.concatenate([fh, fh], axis=0))
                     + dot(ktp[:, :C], fl)
                 )
+            for d in range(per_chunk):
+                to = c * per_chunk + d
+
+                @pl.when(to == me)
+                def _():
+                    hidden_local(s).start()
+
+                @pl.when(to != me)
+                def _():
+                    hidden_copy(s, to, me).start()
+
             return carry
 
         lax.fori_loop(0, count, advance, 0)
+        logit = jnp.sum(sel_ref[s] * probe_ref[me], axis=-1, keepdims=True)
+        part_ref[me, s] = jnp.broadcast_to(logit, (8, C))
         return carry
 
     lax.fori_loop(0, sols, one_solution, 0)
 
-
-def run_layer(ends, owner, qk, v, gate, decay, beta, rate, bias, tqk, tv, init, gain):
+    for r in range(1, shares):
+        part_copy(r, me).start()
+    for r in range(1, shares):
+        part_copy(r, me).wait_send()
+        part_copy(r, lax.rem(me + shares - r, shares)).wait_recv()
+    total = part_ref[0]
+    for other in range(1, shares):
+        total = total + part_ref[other]
+    logit_ref[...] = total
+    for r in range(1, n_sol):
+        state_copy(r, my_sol).wait_send()
+    for s in range(sols):
+        hidden_local(s).wait()
+        for r in range(1, shares):
+            hidden_copy(s, lax.rem(me + r, shares), me).wait_send()
+            other = lax.rem(me + shares - r, shares)
+            hidden_copy(s, other, other).wait_recv()
+
+
+def run_layer(ends, owner, qk, v, gate, decay, beta, rate, bias, tqk, tv, own, gain, probe):
     sols, length, width = v.shape
     groups = width // C // 2
     count = length // C
     shares = lax.axis_size(("head", "sub"))
+    n_sol = lax.axis_size("sol")
     vmem = pl.BlockSpec(memory_space=pltpu.VMEM)
     return pl.pallas_call(
         kernel,
         out_shape=(
-            jax.ShapeDtypeStruct((shares, sols, length // shares, width), BF16),
-            jax.ShapeDtypeStruct((sols, 8, width), F32),
+            jax.ShapeDtypeStruct((sols, length // shares, shares * width), BF16),
+            jax.ShapeDtypeStruct((sols, 8, C), F32),
         ),
-        in_specs=[pl.BlockSpec(memory_space=pltpu.SMEM)] * 2 + [vmem] * 11,
-        out_specs=(vmem, vmem),
+        in_specs=[pl.BlockSpec(memory_space=pltpu.SMEM)] * 2 + [vmem] * 12,
+        out_specs=(pl.BlockSpec(memory_space=pl.ANY), vmem),
         scratch_shapes=[
+            pltpu.VMEM((shares, sols, length // shares, width), BF16),
+            pltpu.VMEM((sols, 8, width), F32),
             pltpu.VMEM((groups, count, 8, C), F32),
             pltpu.VMEM((groups, count, 2 * C, 2 * C), BF16),
             pltpu.VMEM((groups, count, C, 2 * C), BF16),
@@ -209,10 +296,19 @@
             pltpu.VMEM((groups, count, 2, C, 2 * C), BF16),
             pltpu.VMEM((groups, count, C, 2 * C), F32),
             pltpu.VMEM((groups, C, 2 * C), F32),
+            pltpu.VMEM((n_sol * own.shape[0],) + own.shape[1:], BF16),
+            pltpu.VMEM((shares, sols, 8, C), F32),
+            pltpu.SemaphoreType.DMA((n_sol - 1,)),
+            pltpu.SemaphoreType.DMA((n_sol - 1,)),
+            pltpu.SemaphoreType.DMA((sols, shares)),
+            pltpu.SemaphoreType.DMA((sols, shares)),
+            pltpu.SemaphoreType.DMA((shares - 1,)),
+            pltpu.SemaphoreType.DMA((shares - 1,)),
+            pltpu.SemaphoreType.DMA((sols,)),
         ],
-        compiler_params=pltpu.CompilerParams(vmem_limit_bytes=56 * 1024 * 1024),
+        compiler_params=pltpu.CompilerParams(vmem_limit_bytes=56 * 1024 * 1024, collective_id=0, has_side_effects=True),
         name="delta_layer",
-    )(ends, owner, qk, v, gate, decay, beta, rate, bias, tqk, tv, init, gain)
+    )(ends, owner, qk, v, gate, decay, beta, rate, bias, tqk, tv, own, gain, probe)
 
 
 def on_device(
@@ -221,19 +317,15 @@
 ):
     sols, length, _, key_width = query_key.shape
     width = values_in.shape[2]
-    every = lax.all_gather(prompt_states, "sol", axis=0, tiled=True)
-    hidden, chosen = run_layer(
+    shares = lax.axis_size(("head", "sub"))
+    hidden, logits = run_layer(
         step_ends, prompt_of,
         query_key.reshape(sols, length, 2 * key_width),
         values_in, gate_in, decay_in, beta_in, decay_rate[:, None], decay_bias[:, None],
-        conv_qk.reshape(conv_qk.shape[0], 2 * key_width), conv_v, every, norm_gain[None, :],
+        conv_qk.reshape(conv_qk.shape[0], 2 * key_width), conv_v, prompt_states, norm_gain[None, :],
+        probe.astype(F32).reshape(shares, 1, width),
     )
-    me = lax.axis_index(("head", "sub"))
-    part = lax.dynamic_slice_in_dim(probe, me * width, width, 0).astype(F32)
-    logits = lax.psum(jnp.sum(chosen[:, :2] * part, axis=-1), ("head", "sub"))
-    moved = lax.all_to_all(hidden, ("head", "sub"), split_axis=0, concat_axis=0, tiled=True)
-    share = length // hidden.shape[0]
-    return moved.transpose(1, 2, 0, 3).reshape(sols, share, hidden.shape[0] * width), logits
+    return hidden, logits[:, :2, 0]
 
 
 def solution(mesh):

time: 152 us -> 102 us (0.67)
  the two profiles are of different devices: /device:TPU:0 before, /device:TPU:11 now
where the time goes in v2:
time: 102 us
  Pallas kernels  87.2 us (85%)
  local copies, waits for them, and re-layouts  12.9 us (13%)
  other arithmetic  1.3 us (1%)
    pallas_call x1, Pallas kernels, run_layer(): pl.pallas_call(kernel, out_shape=(jax.ShapeDtypeStruct((sols, length // s...  87.2 us
    unnamed x2, local copies, waits for them, and re-layouts  4.44 us
    reshape x1, local copies, waits for them, and re-layouts, on_device(): query_key.reshape(sols, length, 2 * key_width)  4.42 us

profile of v2, /device:TPU:11, one launch (start us, length us, event | category | flops | bytes accessed | tf_op | source)
XLA Modules:
  0.0 102.0 jit_solution(10455984547401058507)
XLA Ops:
  0.6 1.3 %copy.18.rate_ref = f32[8,1]{1,0:T(8,128)} copy(f32[8,1]{0,1:T(1,128)} %bitcast.10) | data formatting | bytes 64 | tf_op jit(solution)/shard_map/broadcast_in_dim | solution.py:324
  1.9 1.3 %copy.19.bias_ref = f32[8,1]{1,0:T(8,128)} copy(f32[8,1]{0,1:T(1,128)} %bitcast.11) | data formatting | bytes 64 | tf_op jit(solution)/shard_map/broadcast_in_dim | solution.py:324
  3.3 1.3 %copy.20 = f32[1,4,2,512]{3,1,2,0:T(4,128)} copy(f32[1,4,2,512]{3,2,1,0:T(2,128)} %bitcast.8) | data formatting | bytes 32768
  4.6 1.3 %reshape.19 = f32[4096]{0:T(1024)} convert(bf16[4096]{0:T(1024)(128)(2,1)} %param.27) | non-fusion elementwise | flops 4096 | bytes 24576 | tf_op jit(solution)/shard_map/reshape | solution.py:326
  5.9 4.4 %reshape.15.qk_ref = bf16[2,512,1024]{2,1,0:T(8,128)(2,1)} reshape(bf16[2,512,2,512]{3,2,1,0:T(2,128)(2,1)} %param.14) | data formatting | bytes 4194304 | tf_op jit(solution)/shard_map/reshape | solution.py:323
  10.3 87.2 %delta_layer.1 = (bf16[2,128,4096]{2,1,0:T(8,128)(2,1)}, f32[2,8,128]{2,1,0:T(8,128)}) custom-call(s32[2,2]{1,0:T(2,128)} %ends_ref.1, s32[2]{0:T(128)} %owner_ref.1, bf16[2,512,1024]{2,1,0:T(8,128)(2,1)} %reshape.15.qk_ref, bf16[2,512,1024]{2,1,0:T(8,128)(2,1)} %v_ref.1, bf16[2,512,1024]{2,1,0:T(8,128)(2,1)} %gate_ref.1, f32[2,8,512]{2,1,0:T(8,128)} %decay_ref.1, ...), custom_call_target="tpu_custom_call" | custom-call | tf_op jit(solution)/shard_map/delta_layer/pallas_call | solution.py:281
  97.5 1.3 %slice_reduce_fusion = f32[2,2]{1,0:T(2,128)} fusion(f32[2,8,128]{2,1,0:T(8,128)} %get-tuple-element.5), kind=kLoop, calls=%fused_computation | loop fusion | bytes 32 | tf_op jit(solution)/shard_map/slice | solution.py:328
  98.9 3.1 %copy.22 = bf16[2,128,4096]{2,1,0:T(8,128)(2,1)} copy(bf16[2,128,4096]{2,1,0:T(8,128)(2,1)} %get-tuple-element.8) | data formatting | bytes 4194304

commit v3 on v2

--- a/solution.py
+++ b/solution.py
@@ -54,7 +54,7 @@
 def kernel(
     ends_ref, owner_ref, qk_ref, v_ref, gate_ref, decay_ref, beta_ref, rate_ref, bias_ref, tqk_ref, tv_ref,
     own_ref, gain_ref, probe_ref, out_ref, logit_ref, hid_ref, sel_ref, rows_ref, kq_ref, kt_ref, x_ref,
-    score_ref, vb_ref, s_ref, every_ref, part_ref, st_send, st_recv, hid_send, hid_recv, lg_send, lg_recv, local_sem,
+    score_ref, vb_ref, s_ref, every_ref, part_ref, mask_ref, st_send, st_recv, hid_send, hid_recv, lg_send, lg_recv, local_sem,
 ):
     sols, length, width = v_ref.shape
     n_sol, n_sub = lax.axis_size("sol"), lax.axis_size("sub")
@@ -112,9 +112,19 @@
     ii = lax.broadcasted_iota(jnp.int32, (C, C), 0)
     jj = lax.broadcasted_iota(jnp.int32, (C, C), 1)
     ones = jnp.where(ii <= jj, 1.0, 0.0).astype(F32)
+    far = ii ^ jj
+    for at, (least, most) in enumerate(((2, 4), (4, 8), (8, 16), (16, 32), (32, 64), (64, 128), (0, 32), (0, 64))):
+        mask = jnp.where((far >= least) & (far < most), 1.0, 0.0).astype(BF16)
+        mask_ref[at] = jnp.concatenate([mask, mask], axis=1)
+    head = lax.broadcasted_iota(jnp.int32, (heads, 1), 0)
+    rate_col = jnp.zeros((heads, 1), F32)
+    bias_col = jnp.zeros((heads, 1), F32)
+    for h in range(heads):
+        rate_col = jnp.where(head == h, rate_ref[h], rate_col)
+        bias_col = jnp.where(head == h, bias_ref[h], bias_col)
 
     def one_solution(s, carry):
-        log_decay = -rate_ref[...] * jax.nn.softplus(decay_ref[s] + bias_ref[...])
+        log_decay = -rate_col * jax.nn.softplus(decay_ref[s] + bias_col)
         beta = jax.nn.sigmoid(beta_ref[s])
         for c in range(count):
             cols = slice(c * C, (c + 1) * C)
@@ -131,8 +141,8 @@
         def prepare(g, carry):
             at = pl.ds(pl.multiple_of(g * C, C), C)
             at2 = pl.ds(pl.multiple_of(width // 2 + g * C, C), C)
-            q = unit(conv_silu(qk_ref[s, :, at].astype(F32), tqk_ref[:, at])) * C ** (-0.5)
-            k = unit(conv_silu(qk_ref[s, :, at2].astype(F32), tqk_ref[:, at2]))
+            q = unit(conv_silu(qk_ref[s, :, at].astype(F32), tqk_ref[:, 0, at])) * C ** (-0.5)
+            k = unit(conv_silu(qk_ref[s, :, at2].astype(F32), tqk_ref[:, 1, at]))
             atv = pl.ds(pl.multiple_of(g * 2 * C, 2 * C), 2 * C)
             v = conv_silu(v_ref[s, :, atv].astype(F32), tv_ref[:, atv])
             systems = []
@@ -154,25 +164,39 @@
                     score_ref[g, c, h] = pack(gram[C:] * weights)
                     systems.append(jnp.where(ii > jj, rate * gram[:C] * weights, 0.0))
                     vb_ref[g, c, :, h * C : (h + 1) * C] = rate * v[span, h * C : (h + 1) * C]
-            far = ii ^ jj
-            eye = jnp.where(ii == jj, 1.0, 0.0)
-            inverses = [eye - jnp.where(far == 1, m, 0.0) for m in systems]
-            b = 2
-            while b < C:
-                near = (far >= b) & (far < 2 * b)
-                packs = [pack(x) for x in inverses]
-                mids = [
-                    packed_dot(p, pack_right(jnp.where(near, m, 0.0)))
-                    for p, m in zip(packs, systems)
-                ]
-                inverses = [
-                    x - packed_dot(pack(y), jnp.concatenate([p, p], axis=0))
-                    for x, y, p in zip(inverses, mids, packs)
-                ]
-                b *= 2
+            parts = [pack(m) for m in systems]
+            wide = [jnp.where((ii ^ jj) == 1, m, 0.0) for m in systems]
+            eye = jnp.where((ii[:32] ^ (jj[:32] & 31)) == 0, 1.0, 0.0)
+            small = [eye - (m[:32] + m[32:64] + m[64:96] + m[96:]) for m in wide]
+
+            def tile(p, at):
+                rows = jnp.concatenate([p] * (C // p.shape[0]), axis=0) * mask_ref[at]
+                return jnp.concatenate([rows, rows], axis=0)
+
+            def near(p, at):
+                rows = p * mask_ref[at]
+                return jnp.concatenate([rows, rows], axis=0)
+
+            for level in range(4):
+                packs = [pack(x) for x in small]
+                mids = [packed_dot(p, near(m, level)) for p, m in zip(packs, parts)]
+                small = [x - packed_dot(pack(y), tile(p, 6)) for x, y, p in zip(small, mids, packs)]
+            half = lax.broadcasted_iota(jnp.int32, (64, C), 0) ^ lax.broadcasted_iota(jnp.int32, (64, C), 1)
+            small = [jnp.where((half & 32) == 0, jnp.concatenate([x, x], axis=0), 0.0) for x in small]
+            packs = [pack(x) for x in small]
+            mids = [packed_dot(p, near(m, 4)) for p, m in zip(packs, parts)]
+            small = [x - packed_dot(pack(y), tile(p, 7)) for x, y, p in zip(small, mids, packs)]
+            packs = [pack(x) for x in small]
+            fulls = [jnp.concatenate([p, p], axis=0) * mask_ref[7] for p in packs]
+            mids = [packed_dot(f[64:], near(m, 5)) for f, m in zip(fulls, parts)]
+            lows = [packed_dot(pack(y), jnp.concatenate([f, f], axis=0)) for y, f in zip(mids, fulls)]
+            inverses = [
+                jnp.concatenate([f[:64], pack(jnp.where(jj[:64] >= 64, x, -y))], axis=0)
+                for f, x, y in zip(fulls, small, lows)
+            ]
             for c in range(count):
                 for h in range(2):
-                    x_ref[g, c, h] = pack(inverses[2 * c + h])
+                    x_ref[g, c, h] = inverses[2 * c + h]
             return carry
 
         lax.fori_loop(0, groups, prepare, 0)
@@ -277,6 +301,7 @@
     count = length // C
     shares = lax.axis_size(("head", "sub"))
     n_sol = lax.axis_size("sol")
+    smem = pl.BlockSpec(memory_space=pltpu.SMEM)
     vmem = pl.BlockSpec(memory_space=pltpu.VMEM)
     return pl.pallas_call(
         kernel,
@@ -284,7 +309,7 @@
             jax.ShapeDtypeStruct((sols, length // shares, shares * width), BF16),
             jax.ShapeDtypeStruct((sols, 8, C), F32),
         ),
-        in_specs=[pl.BlockSpec(memory_space=pltpu.SMEM)] * 2 + [vmem] * 12,
+        in_specs=[smem] * 2 + [vmem] * 5 + [smem] * 2 + [vmem] * 5,
         out_specs=(pl.BlockSpec(memory_space=pl.ANY), vmem),
         scratch_shapes=[
             pltpu.VMEM((shares, sols, length // shares, width), BF16),
@@ -298,6 +323,7 @@
             pltpu.VMEM((groups, C, 2 * C), F32),
             pltpu.VMEM((n_sol * own.shape[0],) + own.shape[1:], BF16),
             pltpu.VMEM((shares, sols, 8, C), F32),
+            pltpu.VMEM((8, C, 2 * C), BF16),
             pltpu.SemaphoreType.DMA((n_sol - 1,)),
             pltpu.SemaphoreType.DMA((n_sol - 1,)),
             pltpu.SemaphoreType.DMA((sols, shares)),
@@ -321,8 +347,8 @@
     hidden, logits = run_layer(
         step_ends, prompt_of,
         query_key.reshape(sols, length, 2 * key_width),
-        values_in, gate_in, decay_in, beta_in, decay_rate[:, None], decay_bias[:, None],
-        conv_qk.reshape(conv_qk.shape[0], 2 * key_width), conv_v, prompt_states, norm_gain[None, :],
+        values_in, gate_in, decay_in, beta_in, decay_rate, decay_bias,
+        conv_qk, conv_v, prompt_states, norm_gain[None, :],
         probe.astype(F32).reshape(shares, 1, width),
     )
     return hidden, logits[:, :2, 0]

time: 102 us -> 99.1 us (0.972)
  local copies, waits for them, and re-layouts: 12.9 us -> 8.9 us
    broadcast_in_dim x2 -> x0, local copies, waits for them, and re-layouts: 2.64 us -> none  [the longest x1 1.32 us: on_device(): decay_bias[:, None]]
    unnamed x2 -> x1, local copies, waits for them, and re-layouts: 4.44 us -> 3.13 us
where the time goes in v3:
time: 99.1 us; the launch traced here: 98.8 us
  Pallas kernels  88 us (89%)
  local copies, waits for them, and re-layouts  8.9 us (9%)
  other arithmetic  1.29 us (1%)
    pallas_call x1, Pallas kernels, run_layer(): pl.pallas_call(kernel, out_shape=(jax.ShapeDtypeStruct((sols, length // s...  88 us
    reshape x1, local copies, waits for them, and re-layouts, on_device(): query_key.reshape(sols, length, 2 * key_width)  4.42 us
    unnamed x1, local copies, waits for them, and re-layouts  3.13 us

profile of v3, /device:TPU:11, one launch (start us, length us, event | category | flops | bytes accessed | tf_op | source)
XLA Modules:
  0.0 98.8 jit_solution(12340879136650281409)
XLA Ops:
  0.6 1.3 %reshape.15 = f32[4096]{0:T(1024)} convert(bf16[4096]{0:T(1024)(128)(2,1)} %param.27) | non-fusion elementwise | flops 4096 | bytes 24576 | tf_op jit(solution)/shard_map/reshape | solution.py:352
  1.9 4.4 %reshape.12.qk_ref = bf16[2,512,1024]{2,1,0:T(8,128)(2,1)} reshape(bf16[2,512,2,512]{3,2,1,0:T(2,128)(2,1)} %param.14) | data formatting | bytes 4194304 | tf_op jit(solution)/shard_map/reshape | solution.py:349
  6.3 88.0 %delta_layer.1 = (bf16[2,128,4096]{2,1,0:T(8,128)(2,1)}, f32[2,8,128]{2,1,0:T(8,128)}) custom-call(s32[2,2]{1,0:T(2,128)} %ends_ref.1, s32[2]{0:T(128)} %owner_ref.1, bf16[2,512,1024]{2,1,0:T(8,128)(2,1)} %reshape.12.qk_ref, bf16[2,512,1024]{2,1,0:T(8,128)(2,1)} %v_ref.1, bf16[2,512,1024]{2,1,0:T(8,128)(2,1)} %gate_ref.1, f32[2,8,512]{2,1,0:T(8,128)} %decay_ref.1, ...), custom_call_target="tpu_custom_call" | custom-call | tf_op jit(solution)/shard_map/delta_layer/pallas_call | solution.py:306
  94.3 1.3 %slice_reduce_fusion = f32[2,2]{1,0:T(2,128)} fusion(f32[2,8,128]{2,1,0:T(8,128)} %get-tuple-element.5), kind=kLoop, calls=%fused_computation | loop fusion | bytes 32 | tf_op jit(solution)/shard_map/slice | solution.py:354
  95.7 3.1 %copy.17 = bf16[2,128,4096]{2,1,0:T(8,128)(2,1)} copy(bf16[2,128,4096]{2,1,0:T(8,128)(2,1)} %get-tuple-element.8) | data formatting | bytes 4194304

commit v4 on v3

--- a/solution.py
+++ b/solution.py
@@ -31,6 +31,13 @@
 
 def packed_dot(left, right):
     both = dot(left, right)
+    return both[:, :C] + both[:, C:]
+
+
+def stacked_dot(left, right):
+    rows = left.shape[0]
+    both = dot(jnp.concatenate([left[:, :C], left[:, C:]], axis=0), right)
+    both = both[:rows] + both[rows:]
     return both[:, :C] + both[:, C:]
 
 
@@ -170,26 +177,24 @@
             small = [eye - (m[:32] + m[32:64] + m[64:96] + m[96:]) for m in wide]
 
             def tile(p, at):
-                rows = jnp.concatenate([p] * (C // p.shape[0]), axis=0) * mask_ref[at]
-                return jnp.concatenate([rows, rows], axis=0)
+                return jnp.concatenate([p] * (C // p.shape[0]), axis=0) * mask_ref[at]
 
             def near(p, at):
-                rows = p * mask_ref[at]
-                return jnp.concatenate([rows, rows], axis=0)
+                return p * mask_ref[at]
 
             for level in range(4):
                 packs = [pack(x) for x in small]
-                mids = [packed_dot(p, near(m, level)) for p, m in zip(packs, parts)]
-                small = [x - packed_dot(pack(y), tile(p, 6)) for x, y, p in zip(small, mids, packs)]
+                mids = [stacked_dot(p, near(m, level)) for p, m in zip(packs, parts)]
+                small = [x - stacked_dot(pack(y), tile(p, 6)) for x, y, p in zip(small, mids, packs)]
             half = lax.broadcasted_iota(jnp.int32, (64, C), 0) ^ lax.broadcasted_iota(jnp.int32, (64, C), 1)
             small = [jnp.where((half & 32) == 0, jnp.concatenate([x, x], axis=0), 0.0) for x in small]
             packs = [pack(x) for x in small]
-            mids = [packed_dot(p, near(m, 4)) for p, m in zip(packs, parts)]
-            small = [x - packed_dot(pack(y), tile(p, 7)) for x, y, p in zip(small, mids, packs)]
+            mids = [stacked_dot(p, near(m, 4)) for p, m in zip(packs, parts)]
+            small = [x - stacked_dot(pack(y), tile(p, 7)) for x, y, p in zip(small, mids, packs)]
             packs = [pack(x) for x in small]
             fulls = [jnp.concatenate([p, p], axis=0) * mask_ref[7] for p in packs]
-            mids = [packed_dot(f[64:], near(m, 5)) for f, m in zip(fulls, parts)]
-            lows = [packed_dot(pack(y), jnp.concatenate([f, f], axis=0)) for y, f in zip(mids, fulls)]
+            mids = [stacked_dot(f[64:], near(m, 5)) for f, m in zip(fulls, parts)]
+            lows = [stacked_dot(pack(y), f) for y, f in zip(mids, fulls)]
             inverses = [
                 jnp.concatenate([f[:64], pack(jnp.where(jj[:64] >= 64, x, -y))], axis=0)
                 for f, x, y in zip(fulls, small, lows)

time: 99.1 us -> 97.7 us (0.986)
  Pallas kernels: 88 us -> 86.6 us
    pallas_call x1, Pallas kernels: 88 us -> 86.6 us  [run_layer(): pl.pallas_call(kernel, out_shape=(jax.ShapeDtypeStruct((sols, length // s...]
where the time goes in v4:
time: 97.7 us; the launch traced here: 97.4 us
  Pallas kernels  86.6 us (89%)
  local copies, waits for them, and re-layouts  8.9 us (9%)
  other arithmetic  1.29 us (1%)
    pallas_call x1, Pallas kernels, run_layer(): pl.pallas_call(kernel, out_shape=(jax.ShapeDtypeStruct((sols, length // s...  86.6 us
    reshape x1, local copies, waits for them, and re-layouts, on_device(): query_key.reshape(sols, length, 2 * key_width)  4.42 us
    unnamed x1, local copies, waits for them, and re-layouts  3.13 us

profile of v4, /device:TPU:11, one launch (start us, length us, event | category | flops | bytes accessed | tf_op | source)
XLA Modules:
  0.0 97.4 jit_solution(9660988567285209497)
XLA Ops:
  0.6 1.3 %reshape.15 = f32[4096]{0:T(1024)} convert(bf16[4096]{0:T(1024)(128)(2,1)} %param.27) | non-fusion elementwise | flops 4096 | bytes 24576 | tf_op jit(solution)/shard_map/reshape | solution.py:357
  1.9 4.4 %reshape.12.qk_ref = bf16[2,512,1024]{2,1,0:T(8,128)(2,1)} reshape(bf16[2,512,2,512]{3,2,1,0:T(2,128)(2,1)} %param.14) | data formatting | bytes 4194304 | tf_op jit(solution)/shard_map/reshape | solution.py:354
  6.3 86.6 %delta_layer.1 = (bf16[2,128,4096]{2,1,0:T(8,128)(2,1)}, f32[2,8,128]{2,1,0:T(8,128)}) custom-call(s32[2,2]{1,0:T(2,128)} %ends_ref.1, s32[2]{0:T(128)} %owner_ref.1, bf16[2,512,1024]{2,1,0:T(8,128)(2,1)} %reshape.12.qk_ref, bf16[2,512,1024]{2,1,0:T(8,128)(2,1)} %v_ref.1, bf16[2,512,1024]{2,1,0:T(8,128)(2,1)} %gate_ref.1, f32[2,8,512]{2,1,0:T(8,128)} %decay_ref.1, ...), custom_call_target="tpu_custom_call" | custom-call | tf_op jit(solution)/shard_map/delta_layer/pallas_call | solution.py:311
  92.9 1.3 %slice_reduce_fusion = f32[2,2]{1,0:T(2,128)} fusion(f32[2,8,128]{2,1,0:T(8,128)} %get-tuple-element.5), kind=kLoop, calls=%fused_computation | loop fusion | bytes 32 | tf_op jit(solution)/shard_map/slice | solution.py:359
  94.3 3.1 %copy.17 = bf16[2,128,4096]{2,1,0:T(8,128)(2,1)} copy(bf16[2,128,4096]{2,1,0:T(8,128)(2,1)} %get-tuple-element.8) | data formatting | bytes 4194304

commit v5 on v4

--- a/solution.py
+++ b/solution.py
@@ -204,7 +204,7 @@
                     x_ref[g, c, h] = inverses[2 * c + h]
             return carry
 
-        lax.fori_loop(0, groups, prepare, 0)
+        lax.fori_loop(0, groups, prepare, 0, unroll=min(2, groups))
 
         @pl.when(s == 0)
         def _():

time: 97.7 us -> 96.2 us (0.985)
  Pallas kernels: 86.6 us -> 85.1 us
    pallas_call x1, Pallas kernels: 86.6 us -> 85.1 us  [run_layer(): pl.pallas_call(kernel, out_shape=(jax.ShapeDtypeStruct((sols, length // s...]
where the time goes in v5:
time: 96.2 us; the launch traced here: 95.9 us
  Pallas kernels  85.1 us (88%)
  local copies, waits for them, and re-layouts  8.9 us (9%)
  other arithmetic  1.29 us (1%)
    pallas_call x1, Pallas kernels, run_layer(): pl.pallas_call(kernel, out_shape=(jax.ShapeDtypeStruct((sols, length // s...  85.1 us
    reshape x1, local copies, waits for them, and re-layouts, on_device(): query_key.reshape(sols, length, 2 * key_width)  4.42 us
    unnamed x1, local copies, waits for them, and re-layouts  3.13 us

profile of v5, /device:TPU:11, one launch (start us, length us, event | category | flops | bytes accessed | tf_op | source)
XLA Modules:
  0.0 95.9 jit_solution(9010690108357784433)
XLA Ops:
  0.6 1.3 %reshape.15 = f32[4096]{0:T(1024)} convert(bf16[4096]{0:T(1024)(128)(2,1)} %param.27) | non-fusion elementwise | flops 4096 | bytes 24576 | tf_op jit(solution)/shard_map/reshape | solution.py:357
  1.9 4.4 %reshape.12.qk_ref = bf16[2,512,1024]{2,1,0:T(8,128)(2,1)} reshape(bf16[2,512,2,512]{3,2,1,0:T(2,128)(2,1)} %param.14) | data formatting | bytes 4194304 | tf_op jit(solution)/shard_map/reshape | solution.py:354
  6.3 85.1 %delta_layer.1 = (bf16[2,128,4096]{2,1,0:T(8,128)(2,1)}, f32[2,8,128]{2,1,0:T(8,128)}) custom-call(s32[2,2]{1,0:T(2,128)} %ends_ref.1, s32[2]{0:T(128)} %owner_ref.1, bf16[2,512,1024]{2,1,0:T(8,128)(2,1)} %reshape.12.qk_ref, bf16[2,512,1024]{2,1,0:T(8,128)(2,1)} %v_ref.1, bf16[2,512,1024]{2,1,0:T(8,128)(2,1)} %gate_ref.1, f32[2,8,512]{2,1,0:T(8,128)} %decay_ref.1, ...), custom_call_target="tpu_custom_call" | custom-call | tf_op jit(solution)/shard_map/delta_layer/pallas_call | solution.py:311
  91.5 1.3 %slice_reduce_fusion = f32[2,2]{1,0:T(2,128)} fusion(f32[2,8,128]{2,1,0:T(8,128)} %get-tuple-element.5), kind=kLoop, calls=%fused_computation | loop fusion | bytes 32 | tf_op jit(solution)/shard_map/slice | solution.py:359
  92.8 3.1 %copy.17 = bf16[2,128,4096]{2,1,0:T(8,128)(2,1)} copy(bf16[2,128,4096]{2,1,0:T(8,128)(2,1)} %get-tuple-element.8) | data formatting | bytes 4194304
